TPU v7x, 32 devices: a whole 2x2x4 slice. The times are simulated.
32 devices in a mesh: dp: 8 (over z, x), mp: 4 (over y, core).
Axes of the slice: x: 2, y: 2, z: 4, core: 2. Of those that a mesh axis runs over, the one named last changes fastest.
Arguments:
- inputs: bfloat16 [24, 2048, 256], P('dp', 'mp'), may hold values from -6 to 6
- segments: int32 [24, 2048], P('dp', 'mp'), may hold values from 0 to 512, as said below
- w_qkv: bfloat16 [3, 256, 256], P(None, None, 'mp'), may hold values from -0.375 to 0.375
- b_qv: bfloat16 [2, 256], P(None, 'mp'), may hold values from -3 to 3
- w_out: bfloat16 [256, 256], P('mp'), may hold values from -2 to 2
- b_out: bfloat16 [256], replicated, may hold values from -3 to 3
- gain_one: float32 [256], replicated, may hold values from 0.1 to 1.9
- shift_one: float32 [256], replicated, may hold values from -2 to 2
- w_in: bfloat16 [256, 512], P(None, 'mp'), may hold values from -0.375 to 0.375
- b_in: bfloat16 [512], P('mp'), may hold values from -3 to 3
- w_back: bfloat16 [512, 256], P('mp'), may hold values from -0.375 to 0.375
- b_back: bfloat16 [256], replicated, may hold values from -3 to 3
- gain_two: float32 [256], replicated, may hold values from 0.1 to 1.9
- shift_two: float32 [256], replicated, may hold values from -2 to 2
- cotangent: bfloat16 [24, 2048, 256], P('dp', 'mp'), may hold values from -6 to 6
Outputs:
- result: bfloat16 [24, 2048, 256], P('dp', 'mp')
- grad_inputs: float32 [24, 2048, 256], P('dp', 'mp')
- grad_qkv: float32 [3, 256, 256], P(None, None, 'mp')
- grad_bias_qv: float32 [2, 256], P(None, 'mp')
- grad_w_out: float32 [256, 256], P('mp')
- grad_b_out: float32 [256], replicated
- grad_gain_one: float32 [256], replicated
- grad_shift_one: float32 [256], replicated
- grad_w_in: float32 [256, 512], P(None, 'mp')
- grad_b_in: float32 [512], P('mp')
- grad_w_back: float32 [512, 256], P('mp')
- grad_b_back: float32 [256], replicated
- grad_gain_two: float32 [256], replicated
- grad_shift_two: float32 [256], replicated
Inputs may be any that keep to these rules, and one draw needn't show every extreme that they name: `segments`: cell numbers start at 0 in every row and never fall along it; in every row one cell covers positions 256 to 1791.
All inputs are finite; a program needn't handle non-finite values.
Results may differ from a plain program's by a relative error of at most 0.017.
Values may be sent and summed in bfloat16 or wider, within the bound.
No kernel may reach another device: no remote copies, remote signals or barrier semaphores. Data moves between devices by JAX's collectives and lax.ppermute only.
A program may use at most 128 MiB of HBM per device.

v0:
```python
import jax
import jax.numpy as jnp
from jax import lax
from jax.sharding import PartitionSpec as P

HEADS = 4


eps = 1e-06


def layer_norm(hidden, gain, shift):
    centre = hidden - jnp.mean(hidden, axis=-1, keepdims=True)
    spread = jnp.mean(centre * centre, axis=-1, keepdims=True)
    return centre * lax.rsqrt(spread + eps) * gain + shift


def gelu_tanh(pre):
    return jax.nn.gelu(pre, approximate=True)


def contract_rows(left, right):
    return lax.dot_general(
        left, right, (((0,), (0,)), ((), ())), preferred_element_type=jnp.float32
    )


def contract_cols(left, right):
    return lax.dot_general(
        left, right, (((1,), (1,)), ((), ())), preferred_element_type=jnp.float32
    )


def masked_scores(query_block, keys, cell_block, cells):
    scale = query_block.shape[-1] ** (-0.5)
    scores = (
        jnp.einsum("qhd,khd->hqk", query_block, keys, preferred_element_type=jnp.float32) * scale
    )
    same = (cell_block[:, None] == cells[None, :])[None]
    return jnp.where(same, scores, -1e30)


def attend_forward(query, keys, values, cells, block):
    length = query.shape[0]
    count = length // block
    q_blocks = query.reshape(count, block, query.shape[1], query.shape[2])
    c_blocks = cells.reshape(count, block)

    def one_block(args):
        query_block, cell_block = args
        scores = masked_scores(query_block, keys, cell_block, cells)
        top = jnp.max(scores, axis=-1, keepdims=True)
        expo = jnp.exp(scores - top)
        total = jnp.sum(expo, axis=-1, keepdims=True)
        probs = (expo / total).astype(jnp.bfloat16)
        out = jnp.einsum("hqk,khd->qhd", probs, values, preferred_element_type=jnp.float32)
        return (out, (top + jnp.log(total))[..., 0])

    outs, lse = lax.map(one_block, (q_blocks, c_blocks))
    return (outs.reshape(query.shape), lse)


def attend_backward(query, keys, values, cells, grad_out, lse, block):
    length = query.shape[0]
    count = length // block
    scale = query.shape[-1] ** (-0.5)
    q_blocks = query.reshape(count, block, query.shape[1], query.shape[2])
    g_blocks = grad_out.reshape(count, block, query.shape[1], query.shape[2])
    c_blocks = cells.reshape(count, block)

    def one_block(carry, args):
        dkeys, dvalues = carry
        query_block, cell_block, grad_block, lse_block = args
        scores = masked_scores(query_block, keys, cell_block, cells)
        probs = jnp.exp(scores - lse_block[..., None])
        dvalues = dvalues + jnp.einsum(
            "hqk,qhd->khd",
            probs.astype(jnp.bfloat16),
            grad_block,
            preferred_element_type=jnp.float32,
        )
        dprobs = jnp.einsum("qhd,khd->hqk", grad_block, values, preferred_element_type=jnp.float32)
        inner = jnp.sum(probs * dprobs, axis=-1, keepdims=True)
        dscores = (probs * (dprobs - inner)).astype(jnp.bfloat16)
        dquery = (
            jnp.einsum("hqk,khd->qhd", dscores, keys, preferred_element_type=jnp.float32) * scale
        )
        dkeys = (
            dkeys
            + jnp.einsum("hqk,qhd->khd", dscores, query_block, preferred_element_type=jnp.float32)
            * scale
        )
        return ((dkeys, dvalues), dquery)

    empty = jnp.zeros(query.shape, jnp.float32)
    (dkeys, dvalues), dquery = lax.scan(
        one_block, (empty, empty), (q_blocks, c_blocks, g_blocks, lse)
    )
    return (dquery.reshape(query.shape), dkeys, dvalues)


def shards(
    inputs,
    segments,
    w_qkv,
    b_qv,
    w_out,
    b_out,
    gain_one,
    shift_one,
    w_in,
    b_in,
    w_back,
    b_back,
    gain_two,
    shift_two,
    cotangent,
):
    seqs, local_len, width = inputs.shape
    head_dim = width // HEADS
    local_width = w_qkv.shape[2]
    heads_here = local_width // head_dim
    whole_in, whole_cells = (
        lax.all_gather(inputs, "mp", axis=1, tiled=True),
        lax.all_gather(segments, "mp", axis=1, tiled=True),
    )
    length = whole_in.shape[1]
    total_rows = seqs * length
    flat_in = whole_in.reshape(total_rows, width)
    bias_stack = jnp.stack(
        [
            b_qv[0].astype(jnp.float32),
            jnp.zeros((local_width,), jnp.float32),
            b_qv[1].astype(jnp.float32),
        ]
    )[:, None, :]
    projected = (
        jnp.einsum("td,cde->cte", flat_in, w_qkv, preferred_element_type=jnp.float32) + bias_stack
    )
    low_qkv = projected.astype(jnp.bfloat16).reshape(3, seqs, length, heads_here, head_dim)
    block = min(512, length)

    def forward_seq(args):
        return attend_forward(args[0], args[1], args[2], args[3], block)

    attended, lse = lax.map(forward_seq, (low_qkv[0], low_qkv[1], low_qkv[2], whole_cells))
    low_att = attended.astype(jnp.bfloat16).reshape(total_rows, local_width)
    partial_att = jnp.dot(low_att, w_out, preferred_element_type=jnp.float32).reshape(
        seqs, length, width
    )
    branch = lax.psum_scatter(
        partial_att.astype(jnp.bfloat16), "mp", scatter_dimension=1, tiled=True
    ).astype(jnp.float32)
    hidden_one = inputs.astype(jnp.float32) + branch + b_out.astype(jnp.float32)
    normed, norm_one_back = jax.vjp(layer_norm, hidden_one, gain_one, shift_one)
    low_normed = normed.astype(jnp.bfloat16)
    w_in_all, b_in_all, w_back_all = (w_in, b_in, w_back)
    feed_rows = lax.all_gather(low_normed, "mp", axis=1, tiled=True).reshape(total_rows, width)
    pre = jnp.dot(feed_rows, w_in_all, preferred_element_type=jnp.float32) + b_in_all.astype(
        jnp.float32
    )
    activated, gelu_back = jax.vjp(gelu_tanh, pre)
    low_act = activated.astype(jnp.bfloat16)
    feed_term = jnp.dot(low_act, w_back_all, preferred_element_type=jnp.float32)
    feed_out = lax.psum_scatter(
        feed_term.reshape(seqs, length, width).astype(jnp.bfloat16),
        "mp",
        scatter_dimension=1,
        tiled=True,
    ).astype(jnp.float32)
    hidden_two = normed + feed_out + b_back.astype(jnp.float32)
    result, norm_two_back = jax.vjp(layer_norm, hidden_two, gain_two, shift_two)
    dh_two, dgain_two, dshift_two = norm_two_back(cotangent.astype(jnp.float32))
    dback_bias = jnp.sum(dh_two, axis=(0, 1))
    low_dz = dh_two.astype(jnp.bfloat16)
    dz_rows = lax.all_gather(low_dz, "mp", axis=1, tiled=True).reshape(total_rows, width)
    dw_back = contract_rows(low_act, dz_rows)
    dact = contract_cols(dz_rows, w_back_all)
    low_dpre = gelu_back(dact)[0].astype(jnp.bfloat16)
    dw_in = contract_rows(feed_rows, low_dpre)
    db_in = jnp.sum(low_dpre.astype(jnp.float32), axis=0)
    dnormed_term = contract_cols(low_dpre, w_in_all)
    dnormed = lax.psum_scatter(
        dnormed_term.reshape(seqs, length, width).astype(jnp.bfloat16),
        "mp",
        scatter_dimension=1,
        tiled=True,
    ).astype(jnp.float32)
    dh_one, dgain_one, dshift_one = norm_one_back(dnormed + dh_two)
    dout_bias = jnp.sum(dh_one, axis=(0, 1))
    low_da = dh_one.astype(jnp.bfloat16)
    da_rows = lax.all_gather(low_da, "mp", axis=1, tiled=True).reshape(total_rows, width)
    dw_out = contract_rows(low_att, da_rows)
    low_dattended = (
        contract_cols(da_rows, w_out)
        .astype(jnp.bfloat16)
        .reshape(seqs, length, heads_here, head_dim)
    )

    def backward_seq(args):
        return attend_backward(args[0], args[1], args[2], args[3], args[4], args[5], block)

    dquery, dkeys, dvalues = lax.map(
        backward_seq, (low_qkv[0], low_qkv[1], low_qkv[2], whole_cells, low_dattended, lse)
    )
    low_dqkv = (
        jnp.stack([dquery, dkeys, dvalues]).astype(jnp.bfloat16).reshape(3, total_rows, local_width)
    )
    dw_qkv = jnp.einsum("td,cte->cde", flat_in, low_dqkv, preferred_element_type=jnp.float32)
    db_qv = jnp.stack(
        [
            jnp.sum(low_dqkv[0].astype(jnp.float32), axis=0),
            jnp.sum(low_dqkv[2].astype(jnp.float32), axis=0),
        ]
    )
    dx_term = jnp.einsum(
        "cte,cde->td", low_dqkv, w_qkv, preferred_element_type=jnp.float32
    ).reshape(seqs, length, width)
    grad_inputs = (
        lax.psum_scatter(
            dx_term.astype(jnp.bfloat16), "mp", scatter_dimension=1, tiled=True
        ).astype(jnp.float32)
        + dh_one
    )
    summed = lax.psum((dw_qkv, db_qv, dw_out, dw_in, db_in, dw_back), "dp")
    shared = lax.psum(
        (dout_bias, dgain_one, dshift_one, dback_bias, dgain_two, dshift_two), ("dp", "mp")
    )
    return (
        result.astype(jnp.bfloat16),
        grad_inputs,
        summed[0],
        summed[1],
        summed[2],
        shared[0],
        shared[1],
        shared[2],
        summed[3],
        summed[4],
        summed[5],
        shared[3],
        shared[4],
        shared[5],
    )


def solution(mesh):
    in_specs = (
        P("dp", "mp", None),
        P("dp", "mp"),
        P(None, None, "mp"),
        P(None, "mp"),
        P("mp", None),
        P(),
        P(),
        P(),
        P(None, "mp"),
        P("mp"),
        P("mp", None),
        P(),
        P(),
        P(),
        P("dp", "mp", None),
    )
    out_specs = (
        P("dp", "mp", None),
        P("dp", "mp", None),
        P(None, None, "mp"),
        P(None, "mp"),
        P("mp", None),
        P(),
        P(),
        P(),
        P(None, "mp"),
        P("mp"),
        P("mp", None),
        P(),
        P(),
        P(),
    )
    return jax.shard_map(shards, mesh=mesh, in_specs=in_specs, out_specs=out_specs, check_vma=False)
```

profile of v0, /device:TPU:0, one launch (start us, length us, event | category | flops | bytes accessed | tf_op | source)
XLA Modules:
  0.0 603.8 jit_solution(15793019614118126018)
XLA Ops:
  8.1 6.4 %all_gather.16 = s32[3,2048]{1,0:T(4,128)S(1)} all-gather(s32[3,512]{1,0:T(4,128)} %param.24), channel_id=1, replica_groups=mesh['dp'=8,'mp'=4] {'mp'}, dimensions={1}, use_global_device_ids=true | all-gather | bytes 30720 | tf_op jit(solution)/shard_map/all_gather | solution.py:125
  15.3 25.6 %all-gather.5.cloned.1.call-done = bf16[3,2048,256]{2,1,0:T(8,128)(2,1)} async-done(((bf16[3,512,256]{2,1,0:T(8,128)(2,1)}), bf16[3,2048,256]{2,1,0:T(8,128)(2,1)}) %all-gather.5.cloned.1.call-update) | async-done | bytes 3145744 | tf_op jit(solution)/shard_map/all_gather | solution.py:124
  53.7 49.8 %while.54 = (s32[]{:T(128)}, bf16[3,2048,1,64]{1,3,2,0:T(8,128)(2,1)}, f32[3,4,1,512]{3,2,1,0:T(1,128)}, bf16[3,2048,1,64]{1,3,2,0:T(8,128)(2,1)S(1)}, s32[3,204...) while((s32[]{:T(128)}, ...), condition=%wide.region_5.6_spmd, body=%wide.region_0.5_spmd.sunk | while | flops 277872128 | bytes 18377040 | solution.py:146
  56.2 11.9 %while.57 = (s32[]{:T(128)}, f32[4,512,1,64]{1,3,2,0:T(8,128)S(1)}, f32[4,1,512]{2,1,0:T(1,128)S(1)}, s32[4,512]{1,0:T(4,128)S(1)}, s32[2048]{0:T(1024)S(1)}, /*...) while((s32[]{:T(128)}, f32[4,512,1,64]{1,3,2,0:T(8,128)S(1)}, ...), condition=%wide.region_4.4_spmd, body=%wide.region_1.3_spmd.sunk | while | flops 277872128 | bytes 13338741 | solution.py:59
  72.8 11.9 %while.57 = (s32[]{:T(128)}, f32[4,512,1,64]{1,3,2,0:T(8,128)S(1)}, f32[4,1,512]{2,1,0:T(1,128)S(1)}, s32[4,512]{1,0:T(4,128)S(1)}, s32[2048]{0:T(1024)S(1)}, /*...) while((s32[]{:T(128)}, f32[4,512,1,64]{1,3,2,0:T(8,128)S(1)}, ...), condition=%wide.region_4.4_spmd, body=%wide.region_1.3_spmd.sunk | while | flops 277872128 | bytes 13338741 | solution.py:59
  89.4 11.9 %while.57 = (s32[]{:T(128)}, f32[4,512,1,64]{1,3,2,0:T(8,128)S(1)}, f32[4,1,512]{2,1,0:T(1,128)S(1)}, s32[4,512]{1,0:T(4,128)S(1)}, s32[2048]{0:T(1024)S(1)}, /*...) while((s32[]{:T(128)}, f32[4,512,1,64]{1,3,2,0:T(8,128)S(1)}, ...), condition=%wide.region_4.4_spmd, body=%wide.region_1.3_spmd.sunk | while | flops 277872128 | bytes 13338741 | solution.py:59
  103.5 4.4 convolution_convert_fusion.3
  108.5 37.5 %reduce-scatter.5.cloned.1.call-done = bf16[3,512,256]{2,1,0:T(8,128)(2,1)} async-done(((bf16[3,2048,256]{2,1,0:T(8,128)(2,1)}), bf16[3,512,256]{2,1,0:T(8,128)(2,1)}) %reduce-scatter.5.cloned.1.call-update) | async-done | bytes 786448 | tf_op jit(solution)/shard_map/reduce_scatter | solution.py:151
  151.0 28.4 %all-gather.7.cloned.1.call-done = bf16[3,2048,256]{2,1,0:T(8,128)(2,1)} async-done(((bf16[3,512,256]{2,1,0:T(8,128)(2,1)}), bf16[3,2048,256]{2,1,0:T(8,128)(2,1)}) %all-gather.7.cloned.1.call-update) | async-done | bytes 3145744 | tf_op jit(solution)/shard_map/all_gather | solution.py:158
  185.9 37.5 %reduce-scatter.7.cloned.1.call-done = bf16[3,512,256]{2,1,0:T(8,128)(2,1)} async-done(((bf16[3,2048,256]{2,1,0:T(8,128)(2,1)}), bf16[3,512,256]{2,1,0:T(8,128)(2,1)}) %reduce-scatter.7.cloned.1.call-update) | async-done | bytes 786448 | tf_op jit(solution)/shard_map/reduce_scatter | solution.py:165
  230.3 28.7 %all-gather.9.cloned.1.call-done = bf16[3,2048,256]{2,1,0:T(8,128)(2,1)} async-done(((bf16[3,512,256]{2,1,0:T(8,128)(2,1)}), bf16[3,2048,256]{2,1,0:T(8,128)(2,1)}) %all-gather.9.cloned.1.call-update) | async-done | bytes 3145744 | tf_op jit(solution)/shard_map/all_gather | solution.py:176
  258.9 5.8 convert_reduce_fusion.1
  267.5 38.1 %reduce-scatter.9.cloned.1.call-done = bf16[3,512,256]{2,1,0:T(8,128)(2,1)} async-done(((bf16[3,2048,256]{2,1,0:T(8,128)(2,1)}), bf16[3,512,256]{2,1,0:T(8,128)(2,1)}) %reduce-scatter.9.cloned.1.call-update) | async-done | bytes 786448 | tf_op jit(solution)/shard_map/reduce_scatter | solution.py:183
  312.9 28.4 %all-gather.11.cloned.1.call-done = bf16[3,2048,256]{2,1,0:T(8,128)(2,1)} async-done(((bf16[3,512,256]{2,1,0:T(8,128)(2,1)}), bf16[3,2048,256]{2,1,0:T(8,128)(2,1)}) %all-gather.11.cloned.1.call-update) | async-done | bytes 3145744 | tf_op jit(solution)/shard_map/all_gather | solution.py:192
  348.9 83.4 %while.56 = (s32[]{:T(128)}, bf16[3,2048,1,64]{3,2,1,0:T(2,128)(2,1)}, bf16[3,2048,1,64]{1,3,2,0:T(8,128)(2,1)}, bf16[3,2048,1,64]{1,3,2,0:T(8,128)(2,1)}, bf16[...) while((s32[]{:T(128)}, ...), condition=%wide.region_21.22_spmd, body=%wide.region_17.21_spmd.sunk | while | flops 682262016 | bytes 43729360 | solution.py:203
  355.3 18.7 %while.58 = (s32[]{:T(128)}, f32[2048,1,64]{0,2,1:T(8,128)S(1)}, f32[2048,1,64]{0,2,1:T(8,128)S(1)}, f32[4,512,1,64]{1,3,2,0:T(8,128)S(1)}, bf16[4,512,1,64]{1,3...) while((s32[]{:T(128)}, f32[2048,1,64]{0,2,1:T(8,128)S(1)}, ...), condition=%wide.region_20.20_spmd.clone, body=%wide.region_18.19_spmd.clone.sunk | while | flops 682262016 | bytes 34758824 | solution.py:96
  383.1 18.7 %while.58 = (s32[]{:T(128)}, f32[2048,1,64]{0,2,1:T(8,128)S(1)}, f32[2048,1,64]{0,2,1:T(8,128)S(1)}, f32[4,512,1,64]{1,3,2,0:T(8,128)S(1)}, bf16[4,512,1,64]{1,3...) while((s32[]{:T(128)}, f32[2048,1,64]{0,2,1:T(8,128)S(1)}, ...), condition=%wide.region_20.20_spmd.clone, body=%wide.region_18.19_spmd.clone.sunk | while | flops 682262016 | bytes 34758824 | solution.py:96
  410.8 18.7 %while.58 = (s32[]{:T(128)}, f32[2048,1,64]{0,2,1:T(8,128)S(1)}, f32[2048,1,64]{0,2,1:T(8,128)S(1)}, f32[4,512,1,64]{1,3,2,0:T(8,128)S(1)}, bf16[4,512,1,64]{1,3...) while((s32[]{:T(128)}, f32[2048,1,64]{0,2,1:T(8,128)S(1)}, ...), condition=%wide.region_20.20_spmd.clone, body=%wide.region_18.19_spmd.clone.sunk | while | flops 682262016 | bytes 34758824 | solution.py:96
  432.3 9.2 %copy.59 = bf16[3,2048,1,64]{1,0,3,2:T(4,128)(2,1)S(1)} copy(bf16[3,2048,1,64]{3,2,1,0:T(2,128)(2,1)} %get-tuple-element.210) | data formatting | bytes 1572864 | tf_op jit(solution)/shard_map/convert.11
  458.8 4.5 fusion.55
  463.3 39.8 %all-reduce = (f32[256]{0:T(256)}, f32[256]{0:T(256)}, f32[256]{0:T(256)}, f32[256]{0:T(256)}, f32[256]{0:T(256)}, /*index=5*/f32[256]{0:T(256)}) all-reduce(f32[256]{0:T(256)S(1)} %copy-done.31, f32[256]{0:T(256)S(1)} %copy-done.28, f32[256]{0:T(256)S(1)} %copy-done.29, ...), channel_id=1, replica_groups=mesh['dp'=8,'mp'=4] {'dp','mp'}, use_global_device_ids=true, to_apply=%region_29.30 | all-reduce | flops 1536 | bytes 12288 | tf_op jit(solution)/shard_map/psum | solution.py:226
  508.9 7.7 %convert_reduce_fusion = f32[64]{0:T(128)S(1)} fusion(bf16[3,2048,1,64]{3,2,1,0:T(2,128)(2,1)} %get-tuple-element.210), kind=kLoop, calls=%fused_computation.78 | loop fusion | flops 786368 | bytes 786688 | tf_op jit(solution)/shard_map/reduce_sum | solution.py:212
  516.9 21.8 %all-reduce.1 = (f32[2,64]{1,0:T(2,128)}, f32[128]{0:T(128)}) all-reduce(f32[2,64]{1,0:T(2,128)S(1)} %pad_maximum_fusion.1, f32[128]{0:T(128)S(1)} %copy-done.37), channel_id=1, replica_groups=mesh['dp'=8,'mp'=4] {'dp'}, use_global_device_ids=true, to_apply=%region_26.27 | all-reduce | flops 256 | bytes 2048 | tf_op jit(solution)/shard_map/psum | solution.py:225
  541.2 49.4 %all-reduce.5.cloned.1.call-done = (f32[3,256,64]{1,2,0:T(8,128)}, f32[64,256]{1,0:T(8,128)}, f32[256,128]{1,0:T(8,128)}, f32[128,256]{1,0:T(8,128)}) async-done(((f32[3,256,64]{1,2,0:T(8,128)}, f32[64,256]{1,0:T(8,128)}, f32[256,128]{1,0:T(8,128)}, f32[128,256]{1,0:T(8,128)}), (f32[3,256,64]{1,2,0:T(8,128)}, f32[64,256]{1,0:T(8,128)}, f32[256,128]{1,0:T(8,128)}, ...) | async-done | bytes 524304 | tf_op jit(solution)/shard_map/psum | solution.py:225
  (421 shorter events, 214.2 us)
Async XLA Ops:
  7.2 33.7 %copy-start = (bf16[3,256,64]{1,2,0:T(8,128)(2,1)S(1)}, bf16[3,256,64]{1,2,0:T(8,128)(2,1)}, u32[]{:S(2)}) copy-start(bf16[3,256,64]{1,2,0:T(8,128)(2,1)} %param.25) | copy-start | bytes 294916
  7.2 33.7 %all-gather.5.cloned.1.call-start = ((), (), s32[]{:S(2)}) async-start(), calls=%async_computation.4 | async-start | bytes 3932160 | tf_op jit(solution)/shard_map/all_gather | solution.py:124
  7.9 138.1 %reduce-scatter.5.cloned.1.call-start = ((), (), s32[]{:S(2)}) async-start(), calls=%async_computation.5 | async-start | bytes 3932160 | tf_op jit(solution)/shard_map/reduce_scatter | solution.py:151
  107.9 38.1 %copy-start.1 = (bf16[3,512,256]{2,1,0:T(8,128)(2,1)S(1)}, bf16[3,512,256]{2,1,0:T(8,128)(2,1)}, u32[]{:S(2)}) copy-start(bf16[3,512,256]{2,1,0:T(8,128)(2,1)} %param.23) | copy-start | bytes 2359300
  107.9 41.4 %copy-start.23 = (f32[256]{0:T(256)S(1)}, f32[256]{0:T(256)}, u32[]{:S(2)}) copy-start(f32[256]{0:T(256)} %param.29) | copy-start | bytes 3076
  107.9 41.4 %copy-start.24 = (f32[256]{0:T(256)S(1)}, f32[256]{0:T(256)}, u32[]{:S(2)}) copy-start(f32[256]{0:T(256)} %param.30) | copy-start | bytes 3076
  108.0 71.5 %all-gather.7.cloned.1.call-start = ((), (), s32[]{:S(2)}) async-start(), calls=%async_computation.6 | async-start | bytes 3932160 | tf_op jit(solution)/shard_map/all_gather | solution.py:158
  147.6 31.9 %copy-start.19 = (bf16[256,128]{1,0:T(8,128)(2,1)S(1)}, bf16[256,128]{1,0:T(8,128)(2,1)}, u32[]{:S(2)}) copy-start(bf16[256,128]{1,0:T(8,128)(2,1)} %param.31) | copy-start | bytes 196612
  150.8 72.6 %reduce-scatter.7.cloned.1.call-start = ((), (), s32[]{:S(2)}) async-start(), calls=%async_computation.7 | async-start | bytes 3932160 | tf_op jit(solution)/shard_map/reduce_scatter | solution.py:165
  185.3 73.7 %all-gather.9.cloned.1.call-start = ((), (), s32[]{:S(2)}) async-start(), calls=%async_computation.8 | async-start | bytes 3932160 | tf_op jit(solution)/shard_map/all_gather | solution.py:176
  185.9 40.0 %copy-start.17 = (bf16[3,512,256]{2,1,0:T(8,128)(2,1)S(1)}, bf16[3,512,256]{2,1,0:T(8,128)(2,1)}, u32[]{:S(2)}) copy-start(bf16[3,512,256]{2,1,0:T(8,128)(2,1)} %param.37) | copy-start | bytes 2359300
  185.9 40.0 %copy-start.25 = (f32[256]{0:T(256)S(1)}, f32[256]{0:T(256)}, u32[]{:S(2)}) copy-start(f32[256]{0:T(256)} %param.35) | copy-start | bytes 3076
  230.2 75.3 %reduce-scatter.9.cloned.1.call-start = ((), (), s32[]{:S(2)}) async-start(), calls=%async_computation.9 | async-start | bytes 3932160 | tf_op jit(solution)/shard_map/reduce_scatter | solution.py:183
  267.4 74.0 %all-gather.11.cloned.1.call-start = ((), (), s32[]{:S(2)}) async-start(), calls=%async_computation.10 | async-start | bytes 3932160 | tf_op jit(solution)/shard_map/all_gather | solution.py:192
  309.8 31.6 %copy-start.20 = (bf16[64,256]{1,0:T(8,128)(2,1)S(1)}, bf16[64,256]{1,0:T(8,128)(2,1)}, u32[]{:S(2)}) copy-start(bf16[64,256]{1,0:T(8,128)(2,1)} %param.27) | copy-start | bytes 98308
  309.8 31.6 %copy-start.21 = (f32[3,512]{1,0:T(4,128)}, f32[3,512]{1,0:T(4,128)S(1)}, u32[]{:S(2)}) copy-start(f32[3,512]{1,0:T(4,128)S(1)} %negate_multiply_fusion) | copy-start | bytes 18436
  312.7 226.0 %reduce-scatter.11.cloned.1.call-start = ((), (), s32[]{:S(2)}) async-start(), calls=%async_computation.11 | async-start | bytes 3932160 | tf_op jit(solution)/shard_map/reduce_scatter | solution.py:220
  432.3 10.3 %copy-start.11 = (bf16[3,2048,1,64]{1,3,2,0:T(8,128)(2,1)S(1)}, bf16[3,2048,1,64]{1,3,2,0:T(8,128)(2,1)}, u32[]{:S(2)}) copy-start(bf16[3,2048,1,64]{1,3,2,0:T(8,128)(2,1)} %get-tuple-element.212) | copy-start | bytes 2359300
  451.7 138.9 %all-reduce.5.cloned.1.call-start = ((), (), s32[]{:S(2)}) async-start(), calls=%async_computation.12 | async-start | bytes 1048576 | tf_op jit(solution)/shard_map/psum | solution.py:225
  458.8 44.4 %copy-start.3 = (bf16[3,2048,256]{2,1,0:T(8,128)(2,1)S(1)}, bf16[3,2048,256]{2,1,0:T(8,128)(2,1)}, u32[]{:S(2)}) copy-start(bf16[3,2048,256]{2,1,0:T(8,128)(2,1)} %all-gather.11.cloned.1.call-done) | copy-start | bytes 9437188
  508.8 7.8 %copy-start.12 = (bf16[3,2048,1,64]{1,3,2,0:T(8,128)(2,1)S(1)}, bf16[3,2048,1,64]{1,3,2,0:T(8,128)(2,1)}, u32[]{:S(2)}) copy-start(bf16[3,2048,1,64]{1,3,2,0:T(8,128)(2,1)} %get-tuple-element.212) | copy-start | bytes 2359300
  508.8 8.0 %copy-start.37 = (f32[128]{0:T(128)S(1)}, f32[128]{0:T(128)}, u32[]{:S(2)}) copy-start(f32[128]{0:T(128)} %get-tuple-element.397) | copy-start | bytes 1540
  508.8 29.8 %copy-start.9 = (f32[3,512,256]{2,1,0:T(8,128)S(1)}, f32[3,512,256]{2,1,0:T(8,128)}, u32[]{:S(2)}) copy-start(f32[3,512,256]{2,1,0:T(8,128)} %copy-done.8) | copy-start | bytes 4718596
  508.9 29.8 %copy-start.22 = (f32[3,512]{1,0:T(4,128)S(1)}, f32[3,512]{1,0:T(4,128)}, u32[]{:S(2)}) copy-start(f32[3,512]{1,0:T(4,128)} %copy-done.21) | copy-start | bytes 18436
  (23 other events, 71.5 us)
Sparse Core Ops, SparseCore 0:
  9.6 31.2 all-gather.4
  108.0 37.9 reduce-scatter.4
  150.9 28.5 all-gather.6
  185.4 37.9 reduce-scatter.6
  230.4 28.5 all-gather.8
  267.5 37.9 reduce-scatter.8
  312.8 28.5 all-gather.10
  451.8 38.3 reduce-scatter.10
  516.7 73.8 all-reduce.4
where the time goes:
time: 613 us; the launch traced here: 604 us
  waiting for transfers between devices  274 us (45%)
  matrix products  117 us (19%)
  local copies, waits for them, and re-layouts  84.3 us (14%)
  blocking collectives  68 us (11%)
  other arithmetic  42.5 us (7%)
  between operations  14.8 us (2%)
    psum x1, waiting for transfers between devices, shards(): summed = lax.psum((dw_qkv, db_qv, dw_out, dw_in, db_in, dw_back), 'dp')  49.4 us
    psum x1, blocking collectives, shards(): lax.psum((dout_bias, dgain_one, dshift_one, dback_bias, dgain_two, dshift...  39.8 us
    reduce_scatter x1, waiting for transfers between devices, shards(): lax.psum_scatter(dnormed_term.reshape(seqs, length, width).astype(jnp.bfl...  38.1 us
    reduce_scatter x1, waiting for transfers between devices, shards(): lax.psum_scatter(partial_att.astype(jnp.bfloat16), 'mp', scatter_dimensio...  37.5 us
    reduce_scatter x1, waiting for transfers between devices, shards(): lax.psum_scatter(feed_term.reshape(seqs, length, width).astype(jnp.bfloat...  37.5 us
    dot_general x24, matrix products, masked_scores(): jnp.einsum('qhd,khd->hqk', query_block, keys, preferred_element_type=jnp....  29.7 us
    all_gather x1, waiting for transfers between devices, shards(): lax.all_gather(low_dz, 'mp', axis=1, tiled=True).reshape(total_rows, width)  28.7 us
    all_gather x1, waiting for transfers between devices, shards(): lax.all_gather(low_normed, 'mp', axis=1, tiled=True)  28.4 us
  transfers between devices with their start and end apart: 9, of which 8 were waited for; matrix products, arithmetic and copies ran while one was open for 5% of the time, Pallas kernels for 0%

commit v1 on v0

v1 whole, which is shorter than its diff:
```python
import functools

import jax
import jax.numpy as jnp
from jax import lax
from jax.experimental import pallas as pl
from jax.experimental.pallas import tpu as pltpu
from jax.sharding import PartitionSpec as P

HEADS = 4
EPS = 1e-06
FAR = -(2.0**99)
GELU_C = 0.7978845608028654
GELU_A = 0.044715

BF = jnp.bfloat16
F32 = jnp.float32

NN = (((1,), (0,)), ((), ()))
NT = (((1,), (1,)), ((), ()))
TN = (((0,), (0,)), ((), ()))

MB = 2**20


def mm(left, right, dims):
    return lax.dot_general(left, right, dims, preferred_element_type=F32)


def vmem():
    return pl.BlockSpec(memory_space=pltpu.VMEM)


def params(limit):
    return pltpu.CompilerParams(vmem_limit_bytes=limit * MB)


def pack_kernel(w_qkv, b_qv, w_out, w_in, b_in, w_back, one, two):
    width = w_qkv.shape[2]
    units = w_in.shape[1]
    for c in range(3):
        one[c * width : (c + 1) * width, :] = w_qkv[c].astype(F32).T.astype(BF)
    one[3 * width :, :] = jnp.zeros((16, one.shape[1]), BF)
    one[3 * width : 3 * width + 1, 0:width] = b_qv[0:1, :]
    one[3 * width : 3 * width + 1, width : 2 * width] = b_qv[1:2, :]
    two[0:width, :] = w_out[...]
    two[width : width + units, :] = w_in[...].astype(F32).T.astype(BF)
    two[width + units : width + 2 * units, :] = w_back[...]
    two[width + 2 * units :, :] = jnp.zeros((16, two.shape[1]), BF)
    two[width + 2 * units : width + 2 * units + 1, 0:units] = b_in[...]


def pack(w_qkv, b_qv, w_out, w_in, b_in, w_back):
    width, units, model = w_qkv.shape[2], w_in.shape[1], w_in.shape[0]
    return pl.pallas_call(
        pack_kernel,
        out_shape=[
            jax.ShapeDtypeStruct((3 * width + 16, model), BF),
            jax.ShapeDtypeStruct((width + 2 * units + 16, model), BF),
        ],
        in_specs=[vmem()] * 6,
        out_specs=[vmem()] * 2,
        name="pack",
    )(w_qkv, b_qv, w_out, w_in, b_in.reshape(1, units), w_back)


def forward_kernel(parts, *refs):
    xs, segs, ws = refs[:parts], refs[parts : 2 * parts], refs[2 * parts : 3 * parts]
    e_out, kt_out, vt_out, qt_out, o_out, stack, feats, qfeat = refs[3 * parts :]
    head = pl.program_id(0)
    here = xs[0].shape[1]
    hd = qt_out.shape[1]

    @pl.when(head == 0)
    def _():
        for b in range(parts):
            stack[b] = ws[b][...]
            seg = segs[b][0]
            lane = lax.broadcasted_iota(jnp.int32, (hd, here), 0)
            digit = jnp.where(lane < 32, jnp.bitwise_and(seg, 31), jnp.right_shift(seg, 5) + 32)
            same = lane == digit
            feats[:, b * here : (b + 1) * here] = jnp.where(same, 0.0, FAR).astype(BF)
            if b == 0:
                qfeat[...] = same.astype(F32)

    w = stack[head]
    bias = w[3 * hd : 3 * hd + 1, 0 : 2 * hd].astype(F32)
    bias = jnp.broadcast_to(bias, (2 * hd, 2 * hd)).T[:, 0:1]
    kt_out[0, hd:, :] = feats[...]
    rows = lax.broadcasted_iota(jnp.int32, (hd, vt_out.shape[2]), 0)
    vt_out[0, hd:, :] = (rows < 2).astype(F32).astype(BF)
    for b in range(parts):
        cols = slice(b * here, (b + 1) * here)
        if b == 0:
            proj = mm(w[: 3 * hd], xs[b][0], NT)
            qt = (proj[:hd] + bias[:hd]).astype(BF).astype(F32) * (hd**-0.5)
            qt_out[0] = qt.astype(BF)
            proj = proj[hd:]
        else:
            proj = mm(w[hd : 3 * hd], xs[b][0], NT)
        kt_out[0, :hd, cols] = proj[:hd].astype(BF)
        vt_out[0, :hd, cols] = (proj[hd:] + bias[hd:]).astype(BF)
    q = jnp.concatenate([qt, qfeat[...]], axis=0).T.astype(BF)
    chunk = here // 2
    for c in range(2):
        rows = slice(c * chunk, (c + 1) * chunk)
        scores = mm(q[rows], kt_out[0], NN)
        top = jnp.max(scores, axis=-1, keepdims=True)
        expo = jnp.exp(scores - top).astype(BF)
        e_out[0, rows, :] = expo
        o_out[0, rows, :] = mm(expo, vt_out[0], NT)


def attend_forward(blocks, segs, ws, heads):
    parts = len(blocks)
    here, model = blocks[0][0].shape[1:]
    length = parts * here
    hd = model // heads

    def row_spec(arr, r):
        return pl.BlockSpec((1,) + arr.shape[1:], lambda h, r=r: (r, 0, 0))

    flops = heads * (4 * here * length * 2 * hd + 4 * length * hd * model)
    return pl.pallas_call(
        functools.partial(forward_kernel, parts),
        grid=(heads,),
        out_shape=[
            jax.ShapeDtypeStruct((heads, here, length), BF),
            jax.ShapeDtypeStruct((heads, 2 * hd, length), BF),
            jax.ShapeDtypeStruct((heads, 2 * hd, length), BF),
            jax.ShapeDtypeStruct((heads, hd, here), BF),
            jax.ShapeDtypeStruct((heads, here, 2 * hd), F32),
        ],
        in_specs=[row_spec(a, r) for a, r in blocks]
        + [row_spec(a, r) for a, r in segs]
        + [pl.BlockSpec(w.shape, lambda h: (0, 0)) for w in ws],
        out_specs=[
            pl.BlockSpec((1, here, length), lambda h: (h, 0, 0)),
            pl.BlockSpec((1, 2 * hd, length), lambda h: (h, 0, 0)),
            pl.BlockSpec((1, 2 * hd, length), lambda h: (h, 0, 0)),
            pl.BlockSpec((1, hd, here), lambda h: (h, 0, 0)),
            pl.BlockSpec((1, here, 2 * hd), lambda h: (h, 0, 0)),
        ],
        scratch_shapes=[
            pltpu.VMEM((parts,) + ws[0].shape, BF),
            pltpu.VMEM((hd, length), BF),
            pltpu.VMEM((hd, here), F32),
        ],
        compiler_params=params(48),
        cost_estimate=pl.CostEstimate(
            flops=flops, bytes_accessed=14 * MB, transcendentals=heads * here * length
        ),
        name="attend_forward",
    )(*[a for a, _ in blocks], *[a for a, _ in segs], *ws)


def middle_kernel(parts, heads, *refs):
    o_in, x_in, cot_in = refs[:3]
    ws = refs[3 : 3 + parts]
    b_out, g_one, e_one, b_back, g_two, e_two, grads_in, sums_in = refs[3 + parts : 11 + parts]
    result_out, dh1_out, do_out, grads_out, sums_out = refs[11 + parts : 16 + parts]
    w_out, w_pad, w_in, w_back = refs[16 + parts :]
    model = x_in.shape[2]
    hd = model // heads
    per = w_out.shape[0] // parts
    units = w_in.shape[0] // parts
    w_pad[...] = jnp.zeros(w_pad.shape, BF)
    bias = []
    for b in range(parts):
        w_out[b * per : (b + 1) * per, :] = ws[b][0:per, :]
        w_pad[b * 2 * per : b * 2 * per + per, :] = ws[b][0:per, :]
        w_in[b * units : (b + 1) * units, :] = ws[b][per : per + units, :]
        w_back[b * units : (b + 1) * units, :] = ws[b][per + units : per + 2 * units, :]
        bias.append(ws[b][per + 2 * units : per + 2 * units + 1, 0:units].astype(F32))
    b_in = jnp.concatenate(bias, axis=1)

    lane = lax.broadcasted_iota(jnp.int32, o_in.shape[1:], 1)
    inv = [1.0 / o_in[h][:, hd : hd + 1] for h in range(heads)]
    normal = [o_in[h] * inv[h] for h in range(heads)]
    tiles = [
        jnp.where(lane < hd, normal[h], pltpu.roll(normal[h + 1], hd, 1))
        for h in range(0, heads, 2)
    ]
    att = jnp.concatenate(tiles, axis=1).astype(BF)
    x = x_in[0].astype(F32)
    h1 = x + mm(att, w_out[...], NN) + b_out[...].astype(F32)

    def norm(h):
        centre = h - jnp.mean(h, axis=-1, keepdims=True)
        rstd = lax.rsqrt(jnp.mean(centre * centre, axis=-1, keepdims=True) + EPS)
        return centre * rstd, rstd

    def norm_back(dy, gain, unit, rstd):
        dn = dy * gain
        mean = jnp.mean(dn, axis=-1, keepdims=True)
        along = jnp.mean(dn * unit, axis=-1, keepdims=True)
        return rstd * (dn - mean - unit * along)

    def down(v):
        return jnp.sum(v, axis=0, keepdims=True)

    n1, rstd1 = norm(h1)
    y1 = n1 * g_one[...] + e_one[...]
    y1b = y1.astype(BF)
    pre = mm(y1b, w_in[...], NT) + b_in
    square = pre * pre
    th = jnp.tanh(GELU_C * pre * (1.0 + GELU_A * square))
    half = 0.5 * (1.0 + th)
    act = (pre * half).astype(BF)
    slope = half + 0.5 * pre * (1.0 - th * th) * (GELU_C * (1.0 + 3.0 * GELU_A * square))
    h2 = y1 + mm(act, w_back[...], NN) + b_back[...].astype(F32)
    n2, rstd2 = norm(h2)
    result_out[0] = (n2 * g_two[...] + e_two[...]).astype(BF)
    cot = cot_in[0].astype(F32)
    dh2 = norm_back(cot, g_two[...], n2, rstd2)
    dz = dh2.astype(BF)
    dact = mm(dz, w_back[...], NT)
    dpre = (dact * slope).astype(BF)
    dw_back = mm(act, dz, TN)
    dw_in = mm(dpre, y1b, TN)
    db_in = down(dpre.astype(F32))
    dy1 = mm(dpre, w_in[...], NN) + dh2
    dh1 = norm_back(dy1, g_one[...], n1, rstd1)
    dh1_out[0] = dh1
    da = dh1.astype(BF)
    dw_out = mm(att, da, TN)
    dwide = mm(da, w_pad[...], NT)
    for h in range(heads):
        grad = (dwide[:, 2 * hd * h : 2 * hd * (h + 1)] * inv[h]).astype(BF)
        wide = grad.astype(F32)
        inner = jnp.sum(wide * normal[h], axis=-1, keepdims=True)
        high = inner.astype(BF).astype(F32)
        rest = inner - high
        wide = jnp.where(lane == hd, -high, jnp.where(lane == hd + 1, -rest, wide))
        do_out[h] = wide.astype(BF)
    for b in range(parts):
        grads_out[b, 0:per, :] = grads_in[b, 0:per, :] + dw_out[b * per : (b + 1) * per]
        here = slice(per, per + units)
        grads_out[b, here, :] = grads_in[b, here, :] + dw_in[b * units : (b + 1) * units]
        here = slice(per + units, per + 2 * units)
        grads_out[b, here, :] = grads_in[b, here, :] + dw_back[b * units : (b + 1) * units]
        grads_out[b, per + 2 * units :, :] = grads_in[b, per + 2 * units :, :]
        here = slice(per + 2 * units, per + 2 * units + 1)
        grads_out[b, here, 0:units] = (
            grads_in[b, here, 0:units] + db_in[:, b * units : (b + 1) * units]
        )
    rows = [down(dh1), down(dy1 * n1), down(dy1), down(dh2), down(cot * n2), down(cot)]
    for i, row in enumerate(rows):
        sums_out[i : i + 1, :] = sums_in[i : i + 1, :] + row
    sums_out[len(rows) :, :] = jnp.zeros((8 - len(rows), model), F32)


def middle(r, o, inputs, cotangent, ws, vectors, grads, sums, heads):
    parts = len(ws)
    here, model = inputs.shape[1:]
    per = grads.shape[1] - 16
    width = model // parts
    units = (per - width) // 2
    row = pl.BlockSpec((1, here, model), lambda i, r=r: (r, 0, 0))
    out_row = pl.BlockSpec((1, here, model), lambda i: (0, 0, 0))

    def whole(a):
        return pl.BlockSpec(a.shape, lambda i, n=len(a.shape): (0,) * n)

    do_shape = jax.ShapeDtypeStruct((heads, here, 2 * (model // heads)), BF)
    return pl.pallas_call(
        functools.partial(middle_kernel, parts, heads),
        grid=(1,),
        out_shape=[
            jax.ShapeDtypeStruct((1, here, model), BF),
            jax.ShapeDtypeStruct((1, here, model), F32),
            do_shape,
            jax.ShapeDtypeStruct(grads.shape, F32),
            jax.ShapeDtypeStruct(sums.shape, F32),
        ],
        in_specs=[whole(o), row, row]
        + [whole(a) for a in ws]
        + [whole(a) for a in vectors]
        + [whole(grads), whole(sums)],
        out_specs=[out_row, out_row, whole(do_shape), whole(grads), whole(sums)],
        scratch_shapes=[
            pltpu.VMEM((parts * width, model), BF),
            pltpu.VMEM((2 * parts * width, model), BF),
            pltpu.VMEM((parts * units, model), BF),
            pltpu.VMEM((parts * units, model), BF),
        ],
        compiler_params=params(48),
        cost_estimate=pl.CostEstimate(
            flops=6 * here * model * (2 * model + 2 * parts * units),
            bytes_accessed=8 * MB,
            transcendentals=here * parts * units,
        ),
        name="middle",
    )(o, inputs, cotangent, *ws, *vectors, grads, sums)


def backward_kernel(parts, heads, *refs):
    e_in, kt_in, vt_in, qt_in, do_in, dh1_in, grads_in = refs[:7]
    xs, ws = refs[7 : 7 + parts], refs[7 + parts : 7 + 2 * parts]
    dxs = refs[7 + 2 * parts : 7 + 3 * parts]
    grads_out, ds, dkv, dq, w_kv, w_q = refs[7 + 3 * parts :]
    head = pl.program_id(0)
    hd = qt_in.shape[1]
    here = do_in.shape[1]
    chunk = here // 2
    for c in range(2):
        rows = slice(c * chunk, (c + 1) * chunk)
        dp = mm(do_in[0, rows, :], vt_in[0], NN)
        ds[rows, :] = (dp * e_in[0, rows, :].astype(F32)).astype(BF)
    dkv[head, hd:, :] = mm(do_in[0], e_in[0], TN)[:hd].astype(BF)
    dkv[head, :hd, :] = mm(qt_in[0], ds[...], NN).astype(BF)
    dq[head] = (mm(kt_in[0, :hd, :], ds[...], NT) * (hd**-0.5)).astype(BF)

    @pl.when(head == heads - 1)
    def _():
        for b in range(parts):
            w_q[b * hd : (b + 1) * hd, :] = ws[b][0:hd, :]
            w_kv[b * 2 * hd : (b + 1) * 2 * hd, :] = ws[b][hd : 3 * hd, :]
        dq_all = dq[...].reshape(heads * hd, here)
        dkv_all = dkv[...].reshape(heads * 2 * hd, parts * here)
        gkv = jnp.zeros((heads * 2 * hd, xs[0].shape[2]), F32)
        for b in range(parts):
            part = dkv_all[:, b * here : (b + 1) * here]
            dx = mm(part, w_kv[...], TN)
            gkv = gkv + mm(part, xs[b][0], NN)
            if b == 0:
                dx = dx + mm(dq_all, w_q[...], TN) + dh1_in[0]
                dxs[b][...] = dx
            else:
                dxs[b][...] = dx.astype(BF)
        gq = mm(dq_all, xs[0][0], NN)
        bq = mm(jnp.ones((8, here), BF), dq_all, NT)
        bkv = mm(jnp.ones((8, parts * here), BF), dkv_all, NT)
        for b in range(parts):
            grads_out[b, 0:hd, :] = grads_in[b, 0:hd, :] + gq[b * hd : (b + 1) * hd]
            grads_out[b, hd : 3 * hd, :] = (
                grads_in[b, hd : 3 * hd, :] + gkv[b * 2 * hd : (b + 1) * 2 * hd]
            )
            grads_out[b, 3 * hd :, :] = grads_in[b, 3 * hd :, :]
            line = slice(3 * hd, 3 * hd + 1)
            grads_out[b, line, 0:hd] = grads_in[b, line, 0:hd] + bq[0:1, b * hd : (b + 1) * hd]
            grads_out[b, line, hd : 2 * hd] = (
                grads_in[b, line, hd : 2 * hd]
                + bkv[0:1, b * 2 * hd + hd : (b + 1) * 2 * hd]
            )


def attend_backward(saved, dh1, grads, blocks, ws, heads):
    e, kt, vt, qt, do = saved
    parts = len(blocks)
    here, model = blocks[0][0].shape[1:]
    hd = model // heads
    length = parts * here

    def per_head(a):
        return pl.BlockSpec((1,) + a.shape[1:], lambda h: (h, 0, 0))

    def whole(a):
        return pl.BlockSpec(a.shape, lambda h, n=len(a.shape): (0,) * n)

    def row_spec(arr, r):
        return pl.BlockSpec((1,) + arr.shape[1:], lambda h, r=r: (r, 0, 0))

    out_shape = [
        jax.ShapeDtypeStruct((here, model), F32 if b == 0 else BF) for b in range(parts)
    ] + [jax.ShapeDtypeStruct(grads.shape, F32)]
    return pl.pallas_call(
        functools.partial(backward_kernel, parts, heads),
        grid=(heads,),
        out_shape=out_shape,
        in_specs=[per_head(a) for a in saved]
        + [whole(dh1), whole(grads)]
        + [row_spec(a, r) for a, r in blocks]
        + [whole(w) for w in ws],
        out_specs=[whole(s) for s in out_shape],
        scratch_shapes=[
            pltpu.VMEM((here, length), BF),
            pltpu.VMEM((heads, 2 * hd, length), BF),
            pltpu.VMEM((heads, hd, here), BF),
            pltpu.VMEM((heads * 2 * hd, model), BF),
            pltpu.VMEM((heads * hd, model), BF),
        ],
        compiler_params=params(48),
        cost_estimate=pl.CostEstimate(
            flops=heads * (8 * here * length * 2 * hd),
            bytes_accessed=16 * MB,
            transcendentals=0,
        ),
        name="attend_backward",
    )(*saved, dh1, grads, *[a for a, _ in blocks], *ws)


def swap(value, axis, size, bit):
    return lax.ppermute(value, axis, [(i, i ^ bit) for i in range(size)])


def bits_of(size):
    return [1 << k for k in range(size.bit_length() - 1)]


def layer(mesh_sizes, *args):
    (inputs, segments, w_qkv, b_qv, w_out, b_out, gain_one, shift_one) = args[:8]
    (w_in, b_in, w_back, b_back, gain_two, shift_two, cotangent) = args[8:]
    dp, mp = mesh_sizes
    rows, here, model = inputs.shape
    heads = HEADS
    width = w_qkv.shape[2]

    def gather(value):
        got = [value]
        for bit in reversed(bits_of(mp)):
            got = got + [swap(g, "mp", mp, bit) for g in got]
        order = [0]
        for bit in reversed(bits_of(mp)):
            order = order + [o ^ bit for o in order]
        return [got[order.index(i)] for i in range(mp)]

    one, two = pack(w_qkv, b_qv, w_out, w_in, b_in, w_back)
    seg_parts = gather(segments.reshape(rows, 1, here))
    w_one = gather(one)
    first = gather(inputs[0:1])
    w_two = gather(two)
    later = gather(inputs[1:]) if rows > 1 else None

    def block_of(r):
        if r == 0:
            return [(inputs, 0)] + [(a, 0) for a in first[1:]]
        return [(inputs, r)] + [(a, r - 1) for a in later[1:]]

    vectors = [
        v.reshape(1, model) for v in (b_out, gain_one, shift_one, b_back, gain_two, shift_two)
    ]
    saved = [
        attend_forward(block_of(r), [(a, r) for a in seg_parts], w_one, heads) for r in range(rows)
    ]
    grads_two = jnp.zeros((mp,) + two.shape, F32)
    sums = jnp.zeros((8, model), F32)
    results, dh1s, dos = [], [], []
    for r in range(rows):
        res, dh1, do, grads_two, sums = middle(
            r, saved[r][4], inputs, cotangent, w_two, vectors, grads_two, sums, heads
        )
        results.append(res)
        dh1s.append(dh1)
        dos.append(do)

    def halve(pieces, bit_list):
        pieces = list(pieces)
        for bit in bit_list:
            keep = {i: p for i, p in pieces_items(pieces) if not i & bit}
            send = {i: p for i, p in pieces_items(pieces) if i & bit}
            for i in keep:
                got = swap(send[i | bit].astype(BF), "mp", mp, bit)
                keep[i] = keep[i].astype(F32) + got.astype(F32)
            pieces = [keep.get(i) for i in range(mp)]
        return pieces[0]

    def pieces_items(pieces):
        return [(i, p) for i, p in enumerate(pieces) if p is not None]

    def over_dp(value):
        for bit in bits_of(dp):
            near = value.astype(BF)
            value = near.astype(F32) + swap(near, "dp", dp, bit).astype(F32)
        return value

    def everywhere(value):
        for bit in bits_of(mp):
            value = value + swap(value, "mp", mp, bit)
        for bit in bits_of(dp):
            value = value + swap(value, "dp", dp, bit)
        return value

    total_two = over_dp(halve([grads_two[i] for i in range(mp)], bits_of(mp)))
    total_sums = everywhere(sums)

    grads_one = jnp.zeros((mp,) + one.shape, F32)
    outs = []
    for r in range(rows):
        out = attend_backward(
            list(saved[r][:4]) + [dos[r]], dh1s[r], grads_one, block_of(r), w_one, heads
        )
        grads_one = out[-1]
        outs.append(halve(out[:-1], bits_of(mp)))
    total_one = over_dp(halve([grads_one[i] for i in range(mp)], bits_of(mp)))

    units = w_in.shape[1]
    return (
        jnp.concatenate(results, axis=0),
        jnp.stack(outs),
        total_one[: 3 * width].reshape(3, width, model).transpose(0, 2, 1),
        total_one[3 * width, : 2 * width].reshape(2, width),
        total_two[:width],
        total_sums[0],
        total_sums[1],
        total_sums[2],
        total_two[width : width + units].T,
        total_two[width + 2 * units, :units],
        total_two[width + units : width + 2 * units],
        total_sums[3],
        total_sums[4],
        total_sums[5],
    )


def solution(mesh):
    in_specs = (
        P("dp", "mp", None),
        P("dp", "mp"),
        P(None, None, "mp"),
        P(None, "mp"),
        P("mp", None),
        P(),
        P(),
        P(),
        P(None, "mp"),
        P("mp"),
        P("mp", None),
        P(),
        P(),
        P(),
        P("dp", "mp", None),
    )
    out_specs = (
        P("dp", "mp", None),
        P("dp", "mp", None),
        P(None, None, "mp"),
        P(None, "mp"),
        P("mp", None),
        P(),
        P(),
        P(),
        P(None, "mp"),
        P("mp"),
        P("mp", None),
        P(),
        P(),
        P(),
    )
    sizes = (mesh.shape["dp"], mesh.shape["mp"])
    return jax.shard_map(
        functools.partial(layer, sizes),
        mesh=mesh,
        in_specs=in_specs,
        out_specs=out_specs,
        check_vma=False,
    )
```

time: 613 us -> 195 us (0.32); the launches traced: 604 us -> 195 us
  waiting for transfers between devices: 274 us -> 50.8 us
  matrix products: 117 us -> 0 us
  Pallas kernels: 0 us -> 84.8 us
  blocking collectives: 68 us -> 0 us
  local copies, waits for them, and re-layouts: 84.3 us -> 18 us
  other arithmetic: 42.5 us -> 4.27 us
  starting transfers between devices: 1 us -> 36.1 us
  between operations: 14.8 us -> 1.06 us
    dot_general x96 -> x0, matrix products: 117 us -> none  [the longest x24 29.7 us: masked_scores(): jnp.einsum('qhd,khd->hqk', query_block, keys, preferred_element_type=jnp....]
    reduce_scatter x4 -> x0, waiting for transfers between devices: 113 us -> none  [the longest x1 38.1 us: shards(): lax.psum_scatter(dnormed_term.reshape(seqs, length, width).astype(jnp.bfl...]
    all_gather x4 -> x0, waiting for transfers between devices: 111 us -> none  [the longest x1 28.7 us: shards(): lax.all_gather(low_dz, 'mp', axis=1, tiled=True).reshape(total_rows, width)]
    pallas_call x0 -> x10, Pallas kernels: none -> 84.8 us  [the longest x3 37.8 us: attend_backward(): pl.pallas_call(functools.partial(backward_kernel, parts, heads), grid=(he...]
    psum x2 -> x0, blocking collectives: 61.6 us -> none  [the longest x1 39.8 us: shards(): lax.psum((dout_bias, dgain_one, dshift_one, dback_bias, dgain_two, dshift...]
    ppermute x0 -> x41, waiting for transfers between devices: none -> 50.8 us  [swap(): return lax.ppermute(value, axis, [(i, i ^ bit) for i in range(size)])]
    psum x1 -> x0, waiting for transfers between devices: 49.4 us -> none  [shards(): summed = lax.psum((dw_qkv, db_qv, dw_out, dw_in, db_in, dw_back), 'dp')]
    ppermute x0 -> x41, starting transfers between devices: none -> 36.1 us  [swap(): return lax.ppermute(value, axis, [(i, i ^ bit) for i in range(size)])]
  transfers between devices with their start and end apart: 9 -> 41, of which waited for: 8 -> 15; matrix products, arithmetic and copies ran while one was open for 5% -> 5% of each run, Pallas kernels for 0% -> 44%
where the time goes in v1:
time: 195 us
  Pallas kernels  84.8 us (43%)
  waiting for transfers between devices  50.8 us (26%)
  starting transfers between devices  36.1 us (19%)
  local copies, waits for them, and re-layouts  18 us (9%)
  other arithmetic  4.27 us (2%)
    ppermute x41, waiting for transfers between devices, swap(): return lax.ppermute(value, axis, [(i, i ^ bit) for i in range(size)])  50.8 us
    pallas_call x3, Pallas kernels, attend_backward(): pl.pallas_call(functools.partial(backward_kernel, parts, heads), grid=(he...  37.8 us
    ppermute x41, starting transfers between devices, swap(): return lax.ppermute(value, axis, [(i, i ^ bit) for i in range(size)])  36.1 us
    pallas_call x3, Pallas kernels, attend_forward(): pl.pallas_call(functools.partial(forward_kernel, parts), grid=(heads,), o...  32.1 us
    pallas_call x3, Pallas kernels, middle(): pl.pallas_call(functools.partial(middle_kernel, parts, heads), grid=(1,),...  13 us
    unnamed x40, local copies, waits for them, and re-layouts  9.84 us
  transfers between devices with their start and end apart: 41, of which 15 were waited for; matrix products, arithmetic and copies ran while one was open for 5% of the time, Pallas kernels for 44%

profile of v1, /device:TPU:0, one launch (start us, length us, event | category | flops | bytes accessed | tf_op | source)
XLA Modules:
  0.0 195.0 jit_solution(7968006515892017298)
XLA Ops:
  1.9 3.0 %collective-permute-start.13 = (bf16[2,512,256]{2,1,0:T(8,128)(2,1)S(1)}, bf16[2,512,256]{2,1,0:T(8,128)(2,1)S(1)}, u32[]{:S(2)}, u32[]{:S(2)}) collective-permute-start(bf16[2,512,256]{2,1,0:T(8,128)(2,1)S(1)} %slice.71), channel_id=1, source_target_pairs={{0,2},{1,3},{2,0},{3,1},{4,6},{5,7},{6,4},{7,5},{8,10},{9,11},{10,... | collective-permute-start | bytes 1572872 | tf_op jit(solution)/shard_map/ppermute | solution.py:394
  8.6 2.0 %collective-permute-start.7 = (bf16[208,256]{1,0:T(8,128)(2,1)}, bf16[208,256]{1,0:T(8,128)(2,1)S(1)}, u32[]{:S(2)}, u32[]{:S(2)}) collective-permute-start(bf16[208,256]{1,0:T(8,128)(2,1)} %get-tuple-element.61.refs_8_.refs_11_), channel_id=1, source_target_pairs={{0,2},{1,3},{2,0},{3,1},{4,6},{5,7},{6,4},{7,5},{8,10},{9,11},{10,... | collective-permute-start | bytes 319496 | tf_op jit(solution)/shard_map/ppermute | solution.py:394
  10.6 12.6 %collective-permute-done.1.refs_2_.refs_9_ = bf16[1,512,256]{2,1,0:T(8,128)(2,1)S(1)} collective-permute-done((bf16[1,512,256]{2,1,0:T(8,128)(2,1)S(1)}, bf16[1,512,256]{2,1,0:T(8,128)(2,1)S(1)}, u32[]{:S(2)}, u32[]{:S(2)}) %collective-permute-start.1) | collective-permute-done | bytes 262176 | tf_op jit(solution)/shard_map/ppermute | solution.py:394
  23.3 2.1 %collective-permute-start.4 = (s32[3,1,512]{2,1,0:T(1,128)S(1)}, s32[3,1,512]{2,1,0:T(1,128)S(1)}, u32[]{:S(2)}, u32[]{:S(2)}) collective-permute-start(s32[3,1,512]{2,1,0:T(1,128)S(1)} %reshape.59.refs_4_), channel_id=1, source_target_pairs={{0,2},{1,3},{2,0},{3,1},{4,6},{5,7},{6,4},{7,5},{8,10},{9,11},{10,... | collective-permute-start | bytes 18440 | tf_op jit(solution)/shard_map/ppermute | solution.py:394
  29.5 2.0 %collective-permute-start.10 = (bf16[336,256]{1,0:T(8,128)(2,1)}, bf16[336,256]{1,0:T(8,128)(2,1)S(1)}, u32[]{:S(2)}, u32[]{:S(2)}) collective-permute-start(bf16[336,256]{1,0:T(8,128)(2,1)} %get-tuple-element.63.refs_3_), channel_id=1, source_target_pairs={{0,2},{1,3},{2,0},{3,1},{4,6},{5,7},{6,4},{7,5},{8,10},{9,11},{10,... | collective-permute-start | bytes 516104 | tf_op jit(solution)/shard_map/ppermute | solution.py:394
  31.7 5.0 %collective-permute-done.10.refs_5_ = bf16[336,256]{1,0:T(8,128)(2,1)S(1)} collective-permute-done((bf16[336,256]{1,0:T(8,128)(2,1)}, bf16[336,256]{1,0:T(8,128)(2,1)S(1)}, u32[]{:S(2)}, u32[]{:S(2)}) %collective-permute-start.10) | collective-permute-done | bytes 172064 | tf_op jit(solution)/shard_map/ppermute | solution.py:394
  38.6 10.7 %attend_forward.3 = (bf16[4,512,2048]{2,1,0:T(8,128)(2,1)}, bf16[4,128,2048]{2,1,0:T(8,128)(2,1)S(1)}, bf16[4,128,2048]{2,1,0:T(8,128)(2,1)}, bf16[4,64,512]{2,1,0:T(8,128)(2,1)S(1)}, f32[4,512,128]{2,1,0:T(8,128)S(1)}) custom-call(bf16[3,512,256]{2,1,0:T(8,128)(2,1)S(1)} %copy-done, bf16[1,512,256]{2,1,0:T(8,128)(2,1)S(1)} %collective-permute-done.refs_1_.refs_8_, ...), custom_call_target="tpu_custom_call" | custom-call | flops 2684354560 | bytes 14680064 | tf_op jit(solution)/shard_map/attend_forward/pallas_call | solution.py:124
  52.0 4.3 %middle.3 = (bf16[1,512,256]{2,1,0:T(8,128)(2,1)S(1)}, f32[1,512,256]{2,1,0:T(8,128)S(1)}, bf16[4,512,128]{2,1,0:T(8,128)(2,1)S(1)}, f32[4,336,256]{2,1,0:T(8,128)S(1)}, f32[8,256]{1,0:T(8,128)S(1)}) custom-call(f32[4,512,128]{2,1,0:T(8,128)S(1)} %get-tuple-element.62.refs_0_, bf16[3,512,256]{2,1,0:T(8,128)(2,1)S(1)} %copy-done, ...), custom_call_target="tpu_custom_call" | custom-call | flops 1207959552 | bytes 8388608 | tf_op jit(solution)/shard_map/middle/pallas_call | solution.py:266
  58.4 12.0 %attend_backward.3 = (f32[512,256]{1,0:T(8,128)S(1)}, bf16[512,256]{1,0:T(8,128)(2,1)S(1)}, bf16[512,256]{1,0:T(8,128)(2,1)S(1)}, bf16[512,256]{1,0:T(8,128)(2,1)S(1)}, f32[4,208,256]{2,1,0:T(8,128)S(1)}) custom-call(bf16[4,512,2048]{2,1,0:T(8,128)(2,1)} %get-tuple-element.73.refs_0_, bf16[4,128,2048]{2,1,0:T(8,128)(2,1)} %copy-done.4, ...), custom_call_target="tpu_custom_call" | custom-call | flops 4294967296 | bytes 16777216 | tf_op jit(solution)/shard_map/attend_backward/pallas_call | solution.py:367
  74.8 10.7 %attend_forward.4 = (bf16[4,512,2048]{2,1,0:T(8,128)(2,1)}, bf16[4,128,2048]{2,1,0:T(8,128)(2,1)S(1)}, bf16[4,128,2048]{2,1,0:T(8,128)(2,1)}, bf16[4,64,512]{2,1,0:T(8,128)(2,1)S(1)}, f32[4,512,128]{2,1,0:T(8,128)S(1)}) custom-call(bf16[3,512,256]{2,1,0:T(8,128)(2,1)S(1)} %copy-done, bf16[2,512,256]{2,1,0:T(8,128)(2,1)S(1)} %collective-permute-done.12.refs_1_.refs_8_, ...), custom_call_target="tpu_custom_call" | custom-call | flops 2684354560 | bytes 14680064 | tf_op jit(solution)/shard_map/attend_forward/pallas_call | solution.py:124
  86.9 10.7 %attend_forward.5 = (bf16[4,512,2048]{2,1,0:T(8,128)(2,1)}, bf16[4,128,2048]{2,1,0:T(8,128)(2,1)S(1)}, bf16[4,128,2048]{2,1,0:T(8,128)(2,1)}, bf16[4,64,512]{2,1,0:T(8,128)(2,1)S(1)}, f32[4,512,128]{2,1,0:T(8,128)S(1)}) custom-call(bf16[3,512,256]{2,1,0:T(8,128)(2,1)S(1)} %copy-done, bf16[2,512,256]{2,1,0:T(8,128)(2,1)S(1)} %collective-permute-done.12.refs_1_.refs_8_, ...), custom_call_target="tpu_custom_call" | custom-call | flops 2684354560 | bytes 14680064 | tf_op jit(solution)/shard_map/attend_forward/pallas_call | solution.py:124
  98.9 4.3 %middle.4 = (bf16[1,512,256]{2,1,0:T(8,128)(2,1)S(1)}, f32[1,512,256]{2,1,0:T(8,128)S(1)}, bf16[4,512,128]{2,1,0:T(8,128)(2,1)S(1)}, f32[4,336,256]{2,1,0:T(8,128)S(1)}, f32[8,256]{1,0:T(8,128)S(1)}) custom-call(f32[4,512,128]{2,1,0:T(8,128)S(1)} %get-tuple-element.65.refs_0_, bf16[3,512,256]{2,1,0:T(8,128)(2,1)S(1)} %copy-done, ...), custom_call_target="tpu_custom_call" | custom-call | flops 1207959552 | bytes 8388608 | tf_op jit(solution)/shard_map/middle/pallas_call | solution.py:266
  104.4 4.3 %middle.5 = (bf16[1,512,256]{2,1,0:T(8,128)(2,1)S(1)}, f32[1,512,256]{2,1,0:T(8,128)S(1)}, bf16[4,512,128]{2,1,0:T(8,128)(2,1)S(1)}, f32[4,336,256]{2,1,0:T(8,128)S(1)}, f32[8,256]{1,0:T(8,128)S(1)}) custom-call(f32[4,512,128]{2,1,0:T(8,128)S(1)} %get-tuple-element.69.refs_0_, bf16[3,512,256]{2,1,0:T(8,128)(2,1)S(1)} %copy-done, ...), custom_call_target="tpu_custom_call" | custom-call | flops 1207959552 | bytes 8388608 | tf_op jit(solution)/shard_map/middle/pallas_call | solution.py:266
  109.5 12.9 %attend_backward.4 = (f32[512,256]{1,0:T(8,128)S(1)}, bf16[512,256]{1,0:T(8,128)(2,1)S(1)}, bf16[512,256]{1,0:T(8,128)(2,1)S(1)}, bf16[512,256]{1,0:T(8,128)(2,1)S(1)}, f32[4,208,256]{2,1,0:T(8,128)}) custom-call(bf16[4,512,2048]{2,1,0:T(8,128)(2,1)} %get-tuple-element.83.refs_0_, bf16[4,128,2048]{2,1,0:T(8,128)(2,1)} %copy-done.3, ...), custom_call_target="tpu_custom_call" | custom-call | flops 4294967296 | bytes 16777216 | tf_op jit(solution)/shard_map/attend_backward/pallas_call | solution.py:367
  122.7 12.9 %attend_backward.5 = (f32[512,256]{1,0:T(8,128)S(1)}, bf16[512,256]{1,0:T(8,128)(2,1)S(1)}, bf16[512,256]{1,0:T(8,128)(2,1)S(1)}, bf16[512,256]{1,0:T(8,128)(2,1)S(1)}, f32[4,208,256]{2,1,0:T(8,128)}) custom-call(bf16[4,512,2048]{2,1,0:T(8,128)(2,1)} %get-tuple-element.94.refs_0_, bf16[4,128,2048]{2,1,0:T(8,128)(2,1)} %copy-done.2, ...), custom_call_target="tpu_custom_call" | custom-call | flops 4294967296 | bytes 16777216 | tf_op jit(solution)/shard_map/attend_backward/pallas_call | solution.py:367
  138.7 1.9 collective-permute-done.38
  144.8 2.8 %collective-permute-start.40 = (f32[8,256]{1,0:T(8,128)S(1)}, f32[8,256]{1,0:T(8,128)S(1)}, u32[]{:S(2)}, u32[]{:S(2)}) collective-permute-start(f32[8,256]{1,0:T(8,128)S(1)} %add.102), channel_id=1, source_target_pairs={{0,16},{4,20},{8,24},{12,28},{16,0},{20,4},{24,8},{28,12},{1,17},{... | collective-permute-start | bytes 24584 | tf_op jit(solution)/shard_map/ppermute | solution.py:394
  152.5 3.0 %collective-permute-done.26 = bf16[208,256]{1,0:T(8,128)(2,1)S(1)} collective-permute-done((bf16[208,256]{1,0:T(8,128)(2,1)S(1)}, bf16[208,256]{1,0:T(8,128)(2,1)S(1)}, u32[]{:S(2)}, u32[]{:S(2)}) %collective-permute-start.26) | collective-permute-done | bytes 106528 | tf_op jit(solution)/shard_map/ppermute | solution.py:394
  159.1 3.5 %collective-permute-done.27 = bf16[208,256]{1,0:T(8,128)(2,1)S(1)} collective-permute-done((bf16[208,256]{1,0:T(8,128)(2,1)S(1)}, bf16[208,256]{1,0:T(8,128)(2,1)S(1)}, u32[]{:S(2)}, u32[]{:S(2)}) %collective-permute-start.27) | collective-permute-done | bytes 106528 | tf_op jit(solution)/shard_map/ppermute | solution.py:394
  166.4 3.1 %collective-permute-done.28 = bf16[208,256]{1,0:T(8,128)(2,1)S(1)} collective-permute-done((bf16[208,256]{1,0:T(8,128)(2,1)S(1)}, bf16[208,256]{1,0:T(8,128)(2,1)S(1)}, u32[]{:S(2)}, u32[]{:S(2)}) %collective-permute-start.28) | collective-permute-done | bytes 106528 | tf_op jit(solution)/shard_map/ppermute | solution.py:394
  171.0 3.9 %collective-permute-done.33 = bf16[336,256]{1,0:T(8,128)(2,1)S(1)} collective-permute-done((bf16[336,256]{1,0:T(8,128)(2,1)S(1)}, bf16[336,256]{1,0:T(8,128)(2,1)S(1)}, u32[]{:S(2)}, u32[]{:S(2)}) %collective-permute-start.33) | collective-permute-done | bytes 172064 | tf_op jit(solution)/shard_map/ppermute | solution.py:394
  174.9 2.6 %collective-permute-start.29 = (bf16[208,256]{1,0:T(8,128)(2,1)S(1)}, bf16[208,256]{1,0:T(8,128)(2,1)S(1)}, u32[]{:S(2)}, u32[]{:S(2)}) collective-permute-start(bf16[208,256]{1,0:T(8,128)(2,1)S(1)} %add_convert_fusion.5), channel_id=1, source_target_pairs={{0,16},{4,20},{8,24},{12,28},{16,0},{20,4},{24,8},{28,12},{1,17},{... | collective-permute-start | bytes 319496 | tf_op jit(solution)/shard_map/ppermute | solution.py:394
  180.6 3.5 %collective-permute-done.34 = bf16[336,256]{1,0:T(8,128)(2,1)S(1)} collective-permute-done((bf16[336,256]{1,0:T(8,128)(2,1)S(1)}, bf16[336,256]{1,0:T(8,128)(2,1)S(1)}, u32[]{:S(2)}, u32[]{:S(2)}) %collective-permute-start.34) | collective-permute-done | bytes 172064 | tf_op jit(solution)/shard_map/ppermute | solution.py:394
  185.6 6.7 %collective-permute-done.35 = bf16[336,256]{1,0:T(8,128)(2,1)S(1)} collective-permute-done((bf16[336,256]{1,0:T(8,128)(2,1)S(1)}, bf16[336,256]{1,0:T(8,128)(2,1)S(1)}, u32[]{:S(2)}, u32[]{:S(2)}) %collective-permute-start.35) | collective-permute-done | bytes 172064 | tf_op jit(solution)/shard_map/ppermute | solution.py:394
  (150 shorter events, 53.1 us)
Async XLA Ops:
  1.9 35.4 %collective-permute-start.13 = (bf16[2,512,256]{2,1,0:T(8,128)(2,1)S(1)}, bf16[2,512,256]{2,1,0:T(8,128)(2,1)S(1)}, u32[]{:S(2)}, u32[]{:S(2)}) collective-permute-start(bf16[2,512,256]{2,1,0:T(8,128)(2,1)S(1)} %slice.71), channel_id=1, source_target_pairs={{0,2},{1,3},{2,0},{3,1},{4,6},{5,7},{6,4},{7,5},{8,10},{9,11},{10,... | collective-permute-start | bytes 1572872 | tf_op jit(solution)/shard_map/ppermute | solution.py:394
  5.9 17.4 %collective-permute-start.1 = (bf16[1,512,256]{2,1,0:T(8,128)(2,1)S(1)}, bf16[1,512,256]{2,1,0:T(8,128)(2,1)S(1)}, u32[]{:S(2)}, u32[]{:S(2)}) collective-permute-start(bf16[1,512,256]{2,1,0:T(8,128)(2,1)S(1)} %slice.70), channel_id=1, source_target_pairs={{0,2},{1,3},{2,0},{3,1},{4,6},{5,7},{6,4},{7,5},{8,10},{9,11},{10,... | collective-permute-start | bytes 786440 | tf_op jit(solution)/shard_map/ppermute | solution.py:394
  8.6 20.9 %collective-permute-start.7 = (bf16[208,256]{1,0:T(8,128)(2,1)}, bf16[208,256]{1,0:T(8,128)(2,1)S(1)}, u32[]{:S(2)}, u32[]{:S(2)}) collective-permute-start(bf16[208,256]{1,0:T(8,128)(2,1)} %get-tuple-element.61.refs_8_.refs_11_), channel_id=1, source_target_pairs={{0,2},{1,3},{2,0},{3,1},{4,6},{5,7},{6,4},{7,5},{8,10},{9,11},{10,... | collective-permute-start | bytes 319496 | tf_op jit(solution)/shard_map/ppermute | solution.py:394
  10.6 26.5 %collective-permute-start = (bf16[1,512,256]{2,1,0:T(8,128)(2,1)S(1)}, bf16[1,512,256]{2,1,0:T(8,128)(2,1)S(1)}, u32[]{:S(2)}, u32[]{:S(2)}) collective-permute-start(bf16[1,512,256]{2,1,0:T(8,128)(2,1)S(1)} %slice.70), channel_id=1, source_target_pairs={{0,1},{1,0},{2,3},{3,2},{4,5},{5,4},{6,7},{7,6},{8,9},{9,8},{10,11... | collective-permute-start | bytes 786440 | tf_op jit(solution)/shard_map/ppermute | solution.py:394
  23.3 14.4 %collective-permute-start.2 = (bf16[1,512,256]{2,1,0:T(8,128)(2,1)S(1)}, bf16[1,512,256]{2,1,0:T(8,128)(2,1)S(1)}, u32[]{:S(2)}, u32[]{:S(2)}) collective-permute-start(bf16[1,512,256]{2,1,0:T(8,128)(2,1)S(1)} %collective-permute-done.1.refs_2_.refs_9_), channel_id=1, source_target_pairs={{0,1},{1,0},{2,3},{3,2},{4,5},{5,4},{6,7},{7,6},{8,9},{9,8},{10,11... | collective-permute-start | bytes 786440 | tf_op jit(solution)/shard_map/ppermute | solution.py:394
  36.6 14.1 %collective-permute-start.9 = (bf16[336,256]{1,0:T(8,128)(2,1)}, bf16[336,256]{1,0:T(8,128)(2,1)S(1)}, u32[]{:S(2)}, u32[]{:S(2)}) collective-permute-start(bf16[336,256]{1,0:T(8,128)(2,1)} %get-tuple-element.63.refs_3_), channel_id=1, source_target_pairs={{0,1},{1,0},{2,3},{3,2},{4,5},{5,4},{6,7},{7,6},{8,9},{9,8},{10,11... | collective-permute-start | bytes 516104 | tf_op jit(solution)/shard_map/ppermute | solution.py:394
  36.6 38.2 %collective-permute-start.12 = (bf16[2,512,256]{2,1,0:T(8,128)(2,1)S(1)}, bf16[2,512,256]{2,1,0:T(8,128)(2,1)S(1)}, u32[]{:S(2)}, u32[]{:S(2)}) collective-permute-start(bf16[2,512,256]{2,1,0:T(8,128)(2,1)S(1)} %slice.71), channel_id=1, source_target_pairs={{0,1},{1,0},{2,3},{3,2},{4,5},{5,4},{6,7},{7,6},{8,9},{9,8},{10,11... | collective-permute-start | bytes 1572872 | tf_op jit(solution)/shard_map/ppermute | solution.py:394
  37.1 13.6 %collective-permute-start.11 = (bf16[336,256]{1,0:T(8,128)(2,1)S(1)}, bf16[336,256]{1,0:T(8,128)(2,1)S(1)}, u32[]{:S(2)}, u32[]{:S(2)}) collective-permute-start(bf16[336,256]{1,0:T(8,128)(2,1)S(1)} %collective-permute-done.10.refs_5_), channel_id=1, source_target_pairs={{0,1},{1,0},{2,3},{3,2},{4,5},{5,4},{6,7},{7,6},{8,9},{9,8},{10,11... | collective-permute-start | bytes 516104 | tf_op jit(solution)/shard_map/ppermute | solution.py:394
  37.2 37.6 %collective-permute-start.14 = (bf16[2,512,256]{2,1,0:T(8,128)(2,1)S(1)}, bf16[2,512,256]{2,1,0:T(8,128)(2,1)S(1)}, u32[]{:S(2)}, u32[]{:S(2)}) collective-permute-start(bf16[2,512,256]{2,1,0:T(8,128)(2,1)S(1)} %collective-permute-done.13.refs_2_.refs_9_), channel_id=1, source_target_pairs={{0,1},{1,0},{2,3},{3,2},{4,5},{5,4},{6,7},{7,6},{8,9},{9,8},{10,11... | collective-permute-start | bytes 1572872 | tf_op jit(solution)/shard_map/ppermute | solution.py:394
  71.4 69.2 %collective-permute-start.15 = (bf16[512,256]{1,0:T(8,128)(2,1)S(1)}, bf16[512,256]{1,0:T(8,128)(2,1)S(1)}, u32[]{:S(2)}, u32[]{:S(2)}) collective-permute-start(bf16[512,256]{1,0:T(8,128)(2,1)S(1)} %get-tuple-element.80), channel_id=1, source_target_pairs={{0,1},{1,0},{2,3},{3,2},{4,5},{5,4},{6,7},{7,6},{8,9},{9,8},{10,11... | collective-permute-start | bytes 786440 | tf_op jit(solution)/shard_map/ppermute | solution.py:394
  73.0 68.2 %collective-permute-start.17 = (bf16[512,256]{1,0:T(8,128)(2,1)S(1)}, bf16[512,256]{1,0:T(8,128)(2,1)S(1)}, u32[]{:S(2)}, u32[]{:S(2)}) collective-permute-start(bf16[512,256]{1,0:T(8,128)(2,1)S(1)} %add_convert_fusion.2), channel_id=1, source_target_pairs={{0,2},{1,3},{2,0},{3,1},{4,6},{5,7},{6,4},{7,5},{8,10},{9,11},{10,... | collective-permute-start | bytes 786440 | tf_op jit(solution)/shard_map/ppermute | solution.py:394
  108.8 41.7 %collective-permute-start.31 = (bf16[336,256]{1,0:T(8,128)(2,1)S(1)}, bf16[336,256]{1,0:T(8,128)(2,1)S(1)}, u32[]{:S(2)}, u32[]{:S(2)}) collective-permute-start(bf16[336,256]{1,0:T(8,128)(2,1)S(1)} %get-tuple-element.123), channel_id=1, source_target_pairs={{0,1},{1,0},{2,3},{3,2},{4,5},{5,4},{6,7},{7,6},{8,9},{9,8},{10,11... | collective-permute-start | bytes 516104 | tf_op jit(solution)/shard_map/ppermute | solution.py:394
  108.9 54.1 %collective-permute-start.30 = (bf16[336,256]{1,0:T(8,128)(2,1)S(1)}, bf16[336,256]{1,0:T(8,128)(2,1)S(1)}, u32[]{:S(2)}, u32[]{:S(2)}) collective-permute-start(bf16[336,256]{1,0:T(8,128)(2,1)S(1)} %get-tuple-element.122), channel_id=1, source_target_pairs={{0,1},{1,0},{2,3},{3,2},{4,5},{5,4},{6,7},{7,6},{8,9},{9,8},{10,11... | collective-permute-start | bytes 516104 | tf_op jit(solution)/shard_map/ppermute | solution.py:394
  109.4 13.0 %collective-permute-start.36 = (f32[8,256]{1,0:T(8,128)S(1)}, f32[8,256]{1,0:T(8,128)S(1)}, u32[]{:S(2)}, u32[]{:S(2)}) collective-permute-start(f32[8,256]{1,0:T(8,128)S(1)} %get-tuple-element.107), channel_id=1, source_target_pairs={{0,1},{1,0},{2,3},{3,2},{4,5},{5,4},{6,7},{7,6},{8,9},{9,8},{10,11... | collective-permute-start | bytes 24584 | tf_op jit(solution)/shard_map/ppermute | solution.py:394
  122.4 14.5 %collective-permute-start.37 = (f32[8,256]{1,0:T(8,128)S(1)}, f32[8,256]{1,0:T(8,128)S(1)}, u32[]{:S(2)}, u32[]{:S(2)}) collective-permute-start(f32[8,256]{1,0:T(8,128)S(1)} %add.99), channel_id=1, source_target_pairs={{0,2},{1,3},{2,0},{3,1},{4,6},{5,7},{6,4},{7,5},{8,10},{9,11},{10,... | collective-permute-start | bytes 24584 | tf_op jit(solution)/shard_map/ppermute | solution.py:394
  140.6 9.3 %collective-permute-start.25 = (bf16[208,256]{1,0:T(8,128)(2,1)S(1)}, bf16[208,256]{1,0:T(8,128)(2,1)S(1)}, u32[]{:S(2)}, u32[]{:S(2)}) collective-permute-start(bf16[208,256]{1,0:T(8,128)(2,1)S(1)} %get-tuple-element.125), channel_id=1, source_target_pairs={{0,1},{1,0},{2,3},{3,2},{4,5},{5,4},{6,7},{7,6},{8,9},{9,8},{10,11... | collective-permute-start | bytes 319496 | tf_op jit(solution)/shard_map/ppermute | solution.py:394
  140.6 11.8 %collective-permute-start.24 = (bf16[208,256]{1,0:T(8,128)(2,1)S(1)}, bf16[208,256]{1,0:T(8,128)(2,1)S(1)}, u32[]{:S(2)}, u32[]{:S(2)}) collective-permute-start(bf16[208,256]{1,0:T(8,128)(2,1)S(1)} %get-tuple-element.124), channel_id=1, source_target_pairs={{0,1},{1,0},{2,3},{3,2},{4,5},{5,4},{6,7},{7,6},{8,9},{9,8},{10,11... | collective-permute-start | bytes 319496 | tf_op jit(solution)/shard_map/ppermute | solution.py:394
  150.0 27.6 %collective-permute-start.18 = (bf16[512,256]{1,0:T(8,128)(2,1)S(1)}, bf16[512,256]{1,0:T(8,128)(2,1)S(1)}, u32[]{:S(2)}, u32[]{:S(2)}) collective-permute-start(bf16[512,256]{1,0:T(8,128)(2,1)S(1)} %get-tuple-element.91), channel_id=1, source_target_pairs={{0,1},{1,0},{2,3},{3,2},{4,5},{5,4},{6,7},{7,6},{8,9},{9,8},{10,11... | collective-permute-start | bytes 786440 | tf_op jit(solution)/shard_map/ppermute | solution.py:394
  155.5 23.7 %collective-permute-start.21 = (bf16[512,256]{1,0:T(8,128)(2,1)S(1)}, bf16[512,256]{1,0:T(8,128)(2,1)S(1)}, u32[]{:S(2)}, u32[]{:S(2)}) collective-permute-start(bf16[512,256]{1,0:T(8,128)(2,1)S(1)} %get-tuple-element.102), channel_id=1, source_target_pairs={{0,1},{1,0},{2,3},{3,2},{4,5},{5,4},{6,7},{7,6},{8,9},{9,8},{10,11... | collective-permute-start | bytes 786440 | tf_op jit(solution)/shard_map/ppermute | solution.py:394
  155.6 9.2 %collective-permute-start.32 = (bf16[336,256]{1,0:T(8,128)(2,1)S(1)}, bf16[336,256]{1,0:T(8,128)(2,1)S(1)}, u32[]{:S(2)}, u32[]{:S(2)}) collective-permute-start(bf16[336,256]{1,0:T(8,128)(2,1)S(1)} %fusion), channel_id=1, source_target_pairs={{0,2},{1,3},{2,0},{3,1},{4,6},{5,7},{6,4},{7,5},{8,10},{9,11},{10,... | collective-permute-start | bytes 516104 | tf_op jit(solution)/shard_map/ppermute | solution.py:394
  162.6 16.5 %collective-permute-start.20 = (bf16[512,256]{1,0:T(8,128)(2,1)S(1)}, bf16[512,256]{1,0:T(8,128)(2,1)S(1)}, u32[]{:S(2)}, u32[]{:S(2)}) collective-permute-start(bf16[512,256]{1,0:T(8,128)(2,1)S(1)} %add_convert_fusion.1), channel_id=1, source_target_pairs={{0,2},{1,3},{2,0},{3,1},{4,6},{5,7},{6,4},{7,5},{8,10},{9,11},{10,... | collective-permute-start | bytes 786440 | tf_op jit(solution)/shard_map/ppermute | solution.py:394
  163.0 16.3 %collective-permute-start.23 = (bf16[512,256]{1,0:T(8,128)(2,1)S(1)}, bf16[512,256]{1,0:T(8,128)(2,1)S(1)}, u32[]{:S(2)}, u32[]{:S(2)}) collective-permute-start(bf16[512,256]{1,0:T(8,128)(2,1)S(1)} %add_convert_fusion), channel_id=1, source_target_pairs={{0,2},{1,3},{2,0},{3,1},{4,6},{5,7},{6,4},{7,5},{8,10},{9,11},{10,... | collective-permute-start | bytes 786440 | tf_op jit(solution)/shard_map/ppermute | solution.py:394
  174.9 9.4 %collective-permute-start.29 = (bf16[208,256]{1,0:T(8,128)(2,1)S(1)}, bf16[208,256]{1,0:T(8,128)(2,1)S(1)}, u32[]{:S(2)}, u32[]{:S(2)}) collective-permute-start(bf16[208,256]{1,0:T(8,128)(2,1)S(1)} %add_convert_fusion.5), channel_id=1, source_target_pairs={{0,16},{4,20},{8,24},{12,28},{16,0},{20,4},{24,8},{28,12},{1,17},{... | collective-permute-start | bytes 319496 | tf_op jit(solution)/shard_map/ppermute | solution.py:394
  184.2 8.2 %collective-permute-start.35 = (bf16[336,256]{1,0:T(8,128)(2,1)S(1)}, bf16[336,256]{1,0:T(8,128)(2,1)S(1)}, u32[]{:S(2)}, u32[]{:S(2)}) collective-permute-start(bf16[336,256]{1,0:T(8,128)(2,1)S(1)} %add_convert_fusion.3), channel_id=1, source_target_pairs={{0,16},{4,20},{8,24},{12,28},{16,0},{20,4},{24,8},{28,12},{1,17},{... | collective-permute-start | bytes 516104 | tf_op jit(solution)/shard_map/ppermute | solution.py:394
  (36 other events, 319.4 us)
